TPU v7x, 32 devices: a whole 2x2x4 slice. The times are simulated.
32 devices in a mesh: circ: 4 (over z), axial: 8 (over y, x, core).
Axes of the slice: x: 2, y: 2, z: 4, core: 2. Of those that a mesh axis runs over, the one named last changes fastest.
Arguments:
- position: float32 [3, 4, 8, 16384], P(None, 'circ', 'axial'), may hold values from -3 to 3
- displacement: float32 [3, 4, 8, 16384], P(None, 'circ', 'axial'), may hold values from -3 to 3
- velocity: float32 [3, 4, 8, 16384], P(None, 'circ', 'axial'), may hold values from -1.5 to 1.5
- bulk: float32 [4, 8, 16384], P('circ', 'axial'), may hold values from 6 to 30
- shear: float32 [4, 8, 16384], P('circ', 'axial'), may hold values from 0.5 to 2
- volume: float32 [4, 8, 16384], P('circ', 'axial'), may hold values from 60 to 200
- edges: int32 [4, 8, 2, 32], P('circ', 'axial'), may hold values from 0 to 127, as said below
- block_pairs: int32 [4, 8, 2, 320], P('circ', 'axial'), may hold values from 0 to 191, as said below
- block_counts: int32 [4, 8, 2], P('circ', 'axial'), may hold values from 128 to 320, as said below
- damage: int32 [4, 8, 320, 128, 128], P('circ', 'axial'), may hold values 0 or 1
Outputs:
- final_displacement: float32 [3, 4, 8, 16384], P(None, 'circ', 'axial')
- final_velocity: float32 [3, 4, 8, 16384], P(None, 'circ', 'axial')
- dilatation: float32 [4, 8, 16384], P('circ', 'axial')
Inputs may be any that keep to these rules, and one draw needn't show every extreme that they name: `edges`: for each device the 64 entries are distinct clusters of that device. `block_pairs`: slot b below 128 pairs cluster b with itself; the further slots below block_counts[c, a, 0] pair two different clusters of the device; the next slots up to block_counts[c, a, 1] are cross blocks whose target is an extended slot of 128 or more, each extended slot of the device's neighbours used exactly once (only the circumferential ones on the last axial section); later slots hold unused pairs of two different local clusters. `block_counts`: entry 0 is the number of local blocks, 128 or more; entry 1 the number of all blocks of the device, which is 32 or 64 more than entry 0.
All inputs are finite; a program needn't handle non-finite values. No bound on the sum of `damage` on one device may be relied on, other than what follows from the above.
Results may differ from a plain program's by a relative error of at most 0.0003.
Values sent between devices are 32-bit elements; how exact they have to be, the bound alone decides.
A program may use at most 64 MiB of HBM per device.

v0:
```python
import jax
import jax.numpy as jnp
from jax import lax
from jax.sharding import PartitionSpec as P

FACING = 32
GROUP_SLOTS = 16
TIME_STEPS = 2


SOFTEN = 0.01
HORIZON_SQ = 1.0
TIMESTEP = 0.07


def from_behind(block, axis, distance):
    devices = range(lax.axis_size(axis))
    route = [((i - distance) % len(devices), i) for i in devices]
    return lax.ppermute(block, axis, route)


def shifted(shard, axis, by):
    size = lax.axis_size(axis)
    pairs = [(i, i + by) for i in range(size) if 0 <= i + by < size]
    return lax.ppermute(shard, axis, pairs)


def bond_geometry(source, target):
    spacing = target[:, 0:3, None, :] - source[:, 0:3, :, None]
    relative = target[:, 3:6, None, :] - source[:, 3:6, :, None]
    stretched = spacing + relative
    length_sq = jnp.sum(spacing * spacing, axis=1)
    deformed_sq = jnp.sum(stretched * stretched, axis=1)
    length = jnp.sqrt(length_sq)
    extension = jnp.sqrt(deformed_sq) - length
    influence = jnp.exp(-length_sq / HORIZON_SQ)
    return (stretched, deformed_sq, length, extension, influence)


def bond_pass(source, target, weight, phase_no):
    stretched, deformed_sq, length, extension, influence = bond_geometry(source, target)
    if phase_no == 1:
        bond_term = weight * influence * length * extension
        return (jnp.sum(bond_term, axis=2)[:, None, :], jnp.sum(bond_term, axis=1)[:, None, :])
    own_state = influence * (
        source[:, 6, :, None] * source[:, 8, :, None] * length + source[:, 7, :, None] * extension
    )
    other_state = influence * (
        target[:, 6, None, :] * target[:, 8, None, :] * length + target[:, 7, None, :] * extension
    )
    magnitude = weight * (own_state + other_state) / jnp.sqrt(deformed_sq + SOFTEN)
    bond_force = magnitude[:, None] * stretched
    return (jnp.sum(bond_force, axis=3), -jnp.sum(bond_force, axis=2))


def sweep_blocks(
    point_table, source_list, target_list, damage_all, begin_slot, finish, phase_no, row_width
):
    extent = point_table.shape[0]
    points = point_table.shape[-1]
    cluster_ids = jnp.arange(extent, dtype=jnp.int32)
    upper_tri = lax.broadcasted_iota(jnp.int32, (points, points), 0) < lax.broadcasted_iota(
        jnp.int32, (points, points), 1
    )

    def turn(group_index, accumulated):
        first_slot = group_index * GROUP_SLOTS
        slot_ids = first_slot + jnp.arange(GROUP_SLOTS, dtype=jnp.int32)
        usable = (slot_ids >= begin_slot) & (slot_ids < finish)
        source_ids = jnp.where(
            usable, lax.dynamic_slice_in_dim(source_list, first_slot, GROUP_SLOTS), 0
        )
        target_ids = jnp.where(
            usable, lax.dynamic_slice_in_dim(target_list, first_slot, GROUP_SLOTS), 0
        )
        damage_slab = lax.dynamic_slice_in_dim(damage_all, first_slot, GROUP_SLOTS)
        keeper = (
            jnp.where((source_ids == target_ids)[:, None, None], upper_tri[None], True)
            & usable[:, None, None]
        )
        weight = jnp.where(
            keeper, damage_slab.astype(jnp.float32), jnp.zeros(damage_slab.shape, jnp.float32)
        )
        source_rows = jnp.take(point_table, source_ids, axis=0)
        target_rows = jnp.take(point_table, target_ids, axis=0)
        source_part, target_part = bond_pass(source_rows, target_rows, weight, phase_no)
        source_hot = (source_ids[:, None] == cluster_ids[None]).astype(jnp.float32)
        target_hot = (target_ids[:, None] == cluster_ids[None]).astype(jnp.float32)
        accumulated = accumulated + jnp.dot(
            source_hot.T,
            source_part.reshape(GROUP_SLOTS, row_width * points),
            precision=lax.Precision.HIGHEST,
            preferred_element_type=jnp.float32,
        )
        accumulated = accumulated + jnp.dot(
            target_hot.T,
            target_part.reshape(GROUP_SLOTS, row_width * points),
            precision=lax.Precision.HIGHEST,
            preferred_element_type=jnp.float32,
        )
        return accumulated

    empty = jnp.zeros((extent, row_width * points), jnp.float32)
    return lax.fori_loop(
        begin_slot // GROUP_SLOTS, (finish + GROUP_SLOTS - 1) // GROUP_SLOTS, turn, empty
    )


def body(
    position, displacement, velocity, bulk, shear, volume, edges, block_pairs, block_counts, damage
):
    points = damage.shape[-1]
    clusters = position.shape[-1] // points

    def clustered(quantity):
        row_count = quantity.shape[0]
        return jnp.transpose(quantity.reshape(row_count, clusters, points), (1, 0, 2))

    def flattened(quantity):
        return jnp.transpose(quantity, (1, 0, 2)).reshape(
            quantity.shape[1], 1, 1, clusters * points
        )

    point_positions = clustered(position)
    moving_state = clustered(displacement)
    velocities = clustered(velocity)
    weighted_volume = clustered(volume)
    bulk_modulus = clustered(bulk)
    shear_modulus = clustered(shear)
    dilatation_factor = (3.0 * bulk_modulus - 5.0 * shear_modulus) / weighted_volume
    deviatoric_factor = 15.0 * shear_modulus / weighted_volume
    circ_ids = edges[0, 0, 0]
    axial_ids = edges[0, 0, 1]
    source_list = block_pairs[0, 0, 0]
    target_list = block_pairs[0, 0, 1]
    total_count = block_counts[0, 0, 1]
    damage_all = damage[0, 0]

    def pull_edges(stacked):
        upward = from_behind(stacked[circ_ids], "circ", -1)
        axially = shifted(stacked[axial_ids], "axial", -1)
        return (upward, axially)

    def push_edges(partials):
        upward = from_behind(partials[clusters : clusters + FACING], "circ", 1)
        axially = shifted(partials[clusters + FACING :], "axial", 1)
        return partials[:clusters].at[circ_ids].add(upward).at[axial_ids].add(axially)

    def evaluate(local_table, upper_table, after_table, phase_no, row_width):
        full_table = jnp.concatenate([local_table, upper_table, after_table], axis=0)
        summed = sweep_blocks(
            full_table, source_list, target_list, damage_all, 0, total_count, phase_no, row_width
        )
        return summed.reshape(summed.shape[0], row_width, points)

    dilatation = jnp.zeros_like(weighted_volume)
    static_point_rows = jnp.concatenate(
        [
            point_positions,
            dilatation_factor,
            deviatoric_factor,
            weighted_volume,
            moving_state,
            velocities,
        ],
        axis=1,
    )
    upper_static, after_static = pull_edges(static_point_rows)
    upper_move, after_move = (upper_static[:, 6:9], after_static[:, 6:9])
    upper_speed, after_speed = (upper_static[:, 9:12], after_static[:, 9:12])
    for step_index in range(TIME_STEPS):
        first_local = jnp.concatenate([point_positions, moving_state], axis=1)
        first_upper = jnp.concatenate([upper_static[:, 0:3], upper_move], axis=1)
        first_after = jnp.concatenate([after_static[:, 0:3], after_move], axis=1)
        partials = evaluate(first_local, first_upper, first_after, 1, 1)
        upper_sum, after_sum = pull_edges(partials[:clusters])
        dilatation = 3.0 * push_edges(partials) / weighted_volume
        upper_theta = (
            3.0 * (partials[clusters : clusters + FACING] + upper_sum) / upper_static[:, 5:6]
        )
        after_theta = 3.0 * (partials[clusters + FACING :] + after_sum) / after_static[:, 5:6]
        second_local_part = jnp.concatenate(
            [point_positions, moving_state, dilatation_factor, deviatoric_factor, dilatation],
            axis=1,
        )
        second_upper = jnp.concatenate(
            [upper_static[:, 0:3], upper_move, upper_static[:, 3:5], upper_theta], axis=1
        )
        second_after = jnp.concatenate(
            [after_static[:, 0:3], after_move, after_static[:, 3:5], after_theta], axis=1
        )
        partials = evaluate(second_local_part, second_upper, second_after, 2, 3)
        upper_sum, after_sum = pull_edges(partials[:clusters])
        force = push_edges(partials)
        upper_force = partials[clusters : clusters + FACING] + upper_sum
        after_force = partials[clusters + FACING :] + after_sum
        velocities = velocities + TIMESTEP * force
        moving_state = moving_state + TIMESTEP * velocities
        upper_speed = upper_speed + TIMESTEP * upper_force
        upper_move = upper_move + TIMESTEP * upper_speed
        after_speed = after_speed + TIMESTEP * after_force
        after_move = after_move + TIMESTEP * after_speed
    return (flattened(moving_state), flattened(velocities), flattened(dilatation)[0])


def solution(mesh):
    placed = (
        P(None, "circ", "axial", None),
        P(None, "circ", "axial", None),
        P(None, "circ", "axial", None),
        P("circ", "axial", None),
        P("circ", "axial", None),
        P("circ", "axial", None),
        P("circ", "axial", None, None),
        P("circ", "axial", None, None),
        P("circ", "axial", None),
        P("circ", "axial", None, None, None),
    )
    return jax.shard_map(
        body,
        mesh=mesh,
        in_specs=placed,
        out_specs=(
            P(None, "circ", "axial", None),
            P(None, "circ", "axial", None),
            P("circ", "axial", None),
        ),
        check_vma=False,
    )
```

profile of v0, /device:TPU:4, one launch (start us, length us, event | category | flops | bytes accessed | tf_op | source)
XLA Modules:
  0.0 783.2 jit_solution(9948848028696974883)
XLA Ops:
  7.8 3.7 collective-permute-start
  19.2 144.6 %while.48 = (s32[]{:T(128)}, f32[192,128]{1,0:T(8,128)S(1)}, s32[]{:T(128)}, s32[]{:T(128)}, s32[320]{0:T(512)S(1)}, /*index=5*/s32[320]{0:T(512)S(1)}, s32[320,...) while((s32[]{:T(128)}, f32[192,128]{1,0:T(8,128)S(1)}, ...), condition=%wide.region_5.7_spmd.clone.clone, body=%wide.region_0.6_spmd.clone.clone.sunk | while | flops 17396116 | bytes 6399283 | solution.py:104
  163.9 3.1 collective-permute-start.3
  168.2 3.6 collective-permute-start.4
  171.7 3.4 collective-permute-start.5
  178.0 208.6 %while.49 = (s32[]{:T(128)}, f32[192,384]{1,0:T(8,128)S(1)}, s32[]{:T(128)}, s32[]{:T(128)}, s32[320]{0:T(512)S(1)}, /*index=5*/s32[320]{0:T(512)S(1)}, s32[320,...) while((s32[]{:T(128)}, f32[192,384]{1,0:T(8,128)S(1)}, ...), condition=%wide.region_13.16_spmd.clone.clone, body=%wide.region_8.15_spmd.clone.clone.sunk | while | flops 42674580 | bytes 9807155 | solution.py:104
  184.7 2.9 fusion.136
  205.6 2.9 fusion.136
  216.0 2.9 fusion.136
  268.1 2.9 fusion.136
  278.5 2.9 fusion.136
  341.1 2.9 fusion.136
  351.5 2.9 fusion.136
  390.5 3.9 collective-permute-start.8
  394.4 4.2 collective-permute-start.9
  403.1 144.7 %while.50 = (s32[]{:T(128)}, f32[192,128]{1,0:T(8,128)S(1)}, s32[]{:T(128)}, s32[]{:T(128)}, s32[320]{0:T(512)S(1)}, /*index=5*/s32[320]{0:T(512)S(1)}, s32[320,...) while((s32[]{:T(128)}, f32[192,128]{1,0:T(8,128)S(1)}, ...), condition=%wide.region_21.24_spmd.clone.clone, body=%wide.region_16.23_spmd.clone.clone.sunk | while | flops 17396116 | bytes 6399283 | solution.py:104
  551.3 3.8 collective-permute-start.12
  555.1 4.2 collective-permute-start.13
  563.1 208.6 %while.51 = (s32[]{:T(128)}, f32[192,384]{1,0:T(8,128)S(1)}, s32[]{:T(128)}, s32[]{:T(128)}, s32[320]{0:T(512)S(1)}, /*index=5*/s32[320]{0:T(512)S(1)}, s32[320,...) while((s32[]{:T(128)}, f32[192,384]{1,0:T(8,128)S(1)}, ...), condition=%wide.region_29.32_spmd.clone.clone, body=%wide.region_24.31_spmd.clone.clone.sunk | while | flops 42674580 | bytes 9807155 | solution.py:104
  580.2 2.9 fusion.151
  632.3 2.9 fusion.151
  642.8 2.9 fusion.151
  694.9 2.9 fusion.151
  774.8 3.0 collective-permute-done.14
  (1598 shorter events, 704.1 us)
Async XLA Ops:
  4.9 172.1 %copy-start.15 = (f32[128,1,128]{2,1,0:T(1,128)}, f32[128,1,128]{2,1,0:T(1,128)S(1)}, u32[]{:S(2)}) copy-start(f32[128,1,128]{2,1,0:T(1,128)S(1)} %get-tuple-element.567) | copy-start | bytes 196612
  4.9 172.1 %copy-start.17 = (f32[128,1,128]{2,1,0:T(1,128)}, f32[128,1,128]{2,1,0:T(1,128)S(1)}, u32[]{:S(2)}) copy-start(f32[128,1,128]{2,1,0:T(1,128)S(1)} %get-tuple-element.568) | copy-start | bytes 196612
  7.8 9.2 %collective-permute-start = (f32[32,12,128]{2,1,0:T(8,128)S(1)}, f32[32,12,128]{2,1,0:T(8,128)S(1)}, u32[]{:S(2)}, u32[]{:S(2)}) collective-permute-start(f32[32,12,128]{2,1,0:T(8,128)S(1)} %gather_fusion.8), channel_id=1, source_target_pairs={{8,0},{16,8},{24,16},{0,24},{9,1},{17,9},{25,17},{1,25},{10,2},{18... | collective-permute-start | bytes 589832 | tf_op jit(solution)/shard_map/ppermute | solution.py:19
  12.1 6.4 collective-permute-start.1
  163.8 11.4 %collective-permute-start.2 = (f32[32,1,128]{2,1,0:T(1,128)S(1)}, f32[32,1,128]{2,1,0:T(1,128)S(1)}, u32[]{:S(2)}, u32[]{:S(2)}) collective-permute-start(f32[32,1,128]{2,1,0:T(1,128)S(1)} %bitcast.169), channel_id=1, source_target_pairs={{24,0},{0,8},{8,16},{16,24},{25,1},{1,9},{9,17},{17,25},{26,2},{2,... | collective-permute-start | bytes 49160 | tf_op jit(solution)/shard_map/ppermute | solution.py:19
  163.9 12.1 %collective-permute-start.3 = (f32[32,1,128]{2,1,0:T(1,128)S(1)}, f32[32,1,128]{2,1,0:T(1,128)S(1)}, u32[]{:S(2)}, u32[]{:S(2)}) collective-permute-start(f32[32,1,128]{2,1,0:T(1,128)S(1)} %bitcast.167), channel_id=1, source_target_pairs={{0,1},{1,2},{2,3},{3,4},{4,5},{5,6},{6,7},{8,9},{9,10},{10,11},{11... | collective-permute-start | bytes 49160 | tf_op jit(solution)/shard_map/ppermute | solution.py:25
  168.2 8.7 %collective-permute-start.4 = (f32[32,1,128]{2,1,0:T(1,128)S(1)}, f32[32,1,128]{2,1,0:T(1,128)S(1)}, u32[]{:S(2)}, u32[]{:S(2)}) collective-permute-start(f32[32,1,128]{2,1,0:T(1,128)S(1)} %bitcast.175), channel_id=1, source_target_pairs={{8,0},{16,8},{24,16},{0,24},{9,1},{17,9},{25,17},{1,25},{10,2},{18... | collective-permute-start | bytes 49160 | tf_op jit(solution)/shard_map/ppermute | solution.py:19
  171.7 5.9 collective-permute-start.5
  178.0 224.0 %copy-start.2 = (f32[3,1,1,16384]{3,2,1,0:T(1,128)S(1)}, f32[3,1,1,16384]{3,2,1,0:T(1,128)}, u32[]{:S(2)}) copy-start(f32[3,1,1,16384]{3,2,1,0:T(1,128)} %param.24) | copy-start | bytes 589828
  178.0 224.0 %copy-start.19 = (f32[3,1,1,16384]{3,2,1,0:T(1,128)S(1)}, f32[3,1,1,16384]{3,2,1,0:T(1,128)}, u32[]{:S(2)}) copy-start(f32[3,1,1,16384]{3,2,1,0:T(1,128)} %param.23) | copy-start | bytes 589828
  386.7 12.0 %collective-permute-start.6 = (f32[32,3,128]{2,1,0:T(4,128)S(1)}, f32[32,3,128]{2,1,0:T(4,128)S(1)}, u32[]{:S(2)}, u32[]{:S(2)}) collective-permute-start(f32[32,3,128]{2,1,0:T(4,128)S(1)} %slice.242), channel_id=1, source_target_pairs={{24,0},{0,8},{8,16},{16,24},{25,1},{1,9},{9,17},{17,25},{26,2},{2,... | collective-permute-start | bytes 147464 | tf_op jit(solution)/shard_map/ppermute | solution.py:19
  386.8 13.5 %collective-permute-start.7 = (f32[32,3,128]{2,1,0:T(4,128)S(1)}, f32[32,3,128]{2,1,0:T(4,128)S(1)}, u32[]{:S(2)}, u32[]{:S(2)}) collective-permute-start(f32[32,3,128]{2,1,0:T(4,128)S(1)} %slice.244), channel_id=1, source_target_pairs={{0,1},{1,2},{2,3},{3,4},{4,5},{5,6},{6,7},{8,9},{9,10},{10,11},{11... | collective-permute-start | bytes 147464 | tf_op jit(solution)/shard_map/ppermute | solution.py:25
  390.5 11.8 %collective-permute-start.8 = (f32[32,3,128]{2,1,0:T(4,128)S(1)}, f32[32,3,128]{2,1,0:T(4,128)S(1)}, u32[]{:S(2)}, u32[]{:S(2)}) collective-permute-start(f32[32,3,128]{2,1,0:T(4,128)S(1)} %gather_fusion.12), channel_id=1, source_target_pairs={{8,0},{16,8},{24,16},{0,24},{9,1},{17,9},{25,17},{1,25},{10,2},{18... | collective-permute-start | bytes 147464 | tf_op jit(solution)/shard_map/ppermute | solution.py:19
  394.4 8.0 %collective-permute-start.9 = (f32[32,3,128]{2,1,0:T(4,128)S(1)}, f32[32,3,128]{2,1,0:T(4,128)S(1)}, u32[]{:S(2)}, u32[]{:S(2)}) collective-permute-start(f32[32,3,128]{2,1,0:T(4,128)S(1)} %gather_fusion.13), channel_id=1, source_target_pairs={{1,0},{2,1},{3,2},{4,3},{5,4},{6,5},{7,6},{9,8},{10,9},{11,10},{12... | collective-permute-start | bytes 147464 | tf_op jit(solution)/shard_map/ppermute | solution.py:25
  547.9 11.5 %collective-permute-start.10 = (f32[32,1,128]{2,1,0:T(1,128)S(1)}, f32[32,1,128]{2,1,0:T(1,128)S(1)}, u32[]{:S(2)}, u32[]{:S(2)}) collective-permute-start(f32[32,1,128]{2,1,0:T(1,128)S(1)} %bitcast.171), channel_id=1, source_target_pairs={{24,0},{0,8},{8,16},{16,24},{25,1},{1,9},{9,17},{17,25},{26,2},{2,... | collective-permute-start | bytes 49160 | tf_op jit(solution)/shard_map/ppermute | solution.py:19
  547.9 12.3 %collective-permute-start.11 = (f32[32,1,128]{2,1,0:T(1,128)S(1)}, f32[32,1,128]{2,1,0:T(1,128)S(1)}, u32[]{:S(2)}, u32[]{:S(2)}) collective-permute-start(f32[32,1,128]{2,1,0:T(1,128)S(1)} %bitcast.165), channel_id=1, source_target_pairs={{0,1},{1,2},{2,3},{3,4},{4,5},{5,6},{6,7},{8,9},{9,10},{10,11},{11... | collective-permute-start | bytes 49160 | tf_op jit(solution)/shard_map/ppermute | solution.py:25
  551.3 9.8 %collective-permute-start.12 = (f32[32,1,128]{2,1,0:T(1,128)S(1)}, f32[32,1,128]{2,1,0:T(1,128)S(1)}, u32[]{:S(2)}, u32[]{:S(2)}) collective-permute-start(f32[32,1,128]{2,1,0:T(1,128)S(1)} %bitcast.176), channel_id=1, source_target_pairs={{8,0},{16,8},{24,16},{0,24},{9,1},{17,9},{25,17},{1,25},{10,2},{18... | collective-permute-start | bytes 49160 | tf_op jit(solution)/shard_map/ppermute | solution.py:19
  555.1 6.7 collective-permute-start.13
  563.0 210.7 %copy-start.6 = (f32[1,1,16384]{2,1,0:T(1,128)S(1)}, f32[1,1,16384]{2,1,0:T(1,128)}, u32[]{:S(2)}) copy-start(f32[1,1,16384]{2,1,0:T(1,128)} %param.27) | copy-start | bytes 196612
  563.0 210.7 %copy-start.24 = (f32[128,128]{1,0:T(8,128)S(1)}, f32[128,128]{1,0:T(8,128)}, u32[]{:S(2)}) copy-start(f32[128,128]{1,0:T(8,128)} %copy-done.23) | copy-start | bytes 196612
  563.1 218.1 %copy-start.1 = (f32[128,3,128]{2,1,0:T(4,128)S(1)}, f32[128,3,128]{2,1,0:T(4,128)}, u32[]{:S(2)}) copy-start(f32[128,3,128]{2,1,0:T(4,128)} %copy-done) | copy-start | bytes 589828
  563.1 218.1 %copy-start.3 = (f32[3,1,1,16384]{3,2,1,0:T(1,128)S(1)}, f32[3,1,1,16384]{3,2,1,0:T(1,128)}, u32[]{:S(2)}) copy-start(f32[3,1,1,16384]{3,2,1,0:T(1,128)} %param.24) | copy-start | bytes 589828
  771.7 6.1 collective-permute-start.14
  771.8 7.7 collective-permute-start.15
  (30 other events, 1627.1 us)
where the time goes:
time: 783 us
  other arithmetic  557 us (71%)
  local copies, waits for them, and re-layouts  108 us (14%)
  matrix products  59.7 us (8%)
  starting transfers between devices  38.4 us (5%)
  loops' own time  11.5 us (1%)
    reduce_sum x80, other arithmetic, bond_geometry(): length_sq = jnp.sum(spacing * spacing, axis=1)  166 us
    reduce_sum x40, other arithmetic, bond_pass(): return (jnp.sum(bond_force, axis=3), -jnp.sum(bond_force, axis=2))  117 us
    div x40, other arithmetic, bond_pass(): weight * (own_state + other_state) / jnp.sqrt(deformed_sq + SOFTEN)  93.3 us
    reduce_sum x40, other arithmetic, bond_pass(): jnp.sum(bond_term, axis=1)[:, None, :]  90.3 us
    eq x80, other arithmetic, turn(): source_ids == target_ids  57.1 us
    gather x80, local copies, waits for them, and re-layouts, turn(): target_rows = jnp.take(point_table, target_ids, axis=0)  45.2 us
    gather x80, local copies, waits for them, and re-layouts, turn(): source_rows = jnp.take(point_table, source_ids, axis=0)  45.2 us
    dot_general x80, matrix products, turn(): jnp.dot(target_hot.T, target_part.reshape(GROUP_SLOTS, row_width * points...  29.9 us
  transfers between devices with their start and end apart: 16, of which 3 were waited for; matrix products, arithmetic and copies ran while one was open for 2% of the time, Pallas kernels for 0%

commit v1 on v0

v1 whole, which is shorter than its diff:
```python
import functools
import math

import jax
import jax.numpy as jnp
from jax import lax
from jax.experimental import pallas as pl
from jax.experimental.pallas import tpu as pltpu
from jax.sharding import PartitionSpec as P

TIME_STEPS = 2
SOFTEN = 0.01
TIMESTEP = 0.07
LOG2E = math.log2(math.e)
SCALE = math.sqrt(LOG2E)
TINY = 1e-12
GROUP = 16
UNROLL = 4


def from_behind(block, axis, distance):
    size = lax.axis_size(axis)
    return lax.ppermute(block, axis, [((i - distance) % size, i) for i in range(size)])


def shifted(shard, axis, by):
    size = lax.axis_size(axis)
    pairs = [(i, i + by) for i in range(size) if 0 <= i + by < size]
    return lax.ppermute(shard, axis, pairs)


def split3(x):
    high = x.astype(jnp.bfloat16).astype(jnp.float32)
    mid = (x - high).astype(jnp.bfloat16).astype(jnp.float32)
    return [high, mid, x - high - mid]


def distance_features(vector):
    parts = [split3(x) for x in vector]
    high, mid, low = ([p[k] for p in parts] for k in range(3))
    norm = split3(vector[0] * vector[0] + vector[1] * vector[1] + vector[2] * vector[2])
    ones = [jnp.ones_like(vector[0])] * 3
    left = [-2.0 * x for x in high * 3] + norm + [-2.0 * x for x in mid * 2 + low] + ones
    right = high + mid + low + ones + high + mid + high + norm
    return left, right


def sum_features(value):
    parts = split3(value)
    ones = [jnp.ones_like(value)] * 3
    pad = [jnp.zeros_like(value)] * 2
    return parts + ones + pad, ones + parts + pad


def halves(x):
    high = x.astype(jnp.bfloat16)
    low = (x - high.astype(jnp.float32)).astype(jnp.bfloat16)
    return high, low


def pair_product(left, right_a, right_b):
    upper = jnp.concatenate([right_a, jnp.zeros_like(right_a)], axis=1)
    lower = jnp.concatenate([jnp.zeros_like(right_b), right_b], axis=1)
    both = jnp.concatenate([upper, lower], axis=0).astype(jnp.bfloat16)
    return lax.dot_general(
        left.astype(jnp.bfloat16),
        both,
        (((0,), (0,)), ((), ())),
        preferred_element_type=jnp.float32,
    )


def pass_kernel(force, first, pairs_ref, count_ref, weight_ref, place_ref, current_ref, *rest):
    rest = list(rest)
    coef_ref = rest.pop(0) if force else None
    out_ref = rest.pop(0)
    kept_ref = rest.pop(0) if first else None
    left_ref, right_ref, acc_ref = rest
    step = pl.program_id(0)
    total = count_ref[1]
    pts = weight_ref.shape[-1]
    extent = place_ref.shape[1]
    width = left_ref.shape[0] // extent
    depth = 16 if force else 8
    rows = 32

    @pl.when(step == 0)
    def _():
        acc_ref[...] = jnp.zeros(acc_ref.shape, jnp.float32)

        def fill(chunk, carry):
            at = pl.ds(pl.multiple_of(chunk * 8, 8), 8)
            groups = [distance_features([place_ref[k, at, :] for k in range(3)])]
            if force:
                groups.append(sum_features(coef_ref[0, at, :]))
            groups.append(distance_features([current_ref[k, at, :] for k in range(3)]))
            if force:
                groups.append(sum_features(coef_ref[1, at, :]))
            left = [x for group in groups for x in group[0]]
            right = [x for group in groups for x in group[1]]
            for k in range(width):
                spot = pl.ds(chunk * (8 * width) + k, 8, stride=width)
                left_ref[spot, :] = left[k]
                right_ref[spot, :] = right[k]
            return carry

        lax.fori_loop(0, extent // 8, fill, 0)

    def one_slot(at):
        slot = step * GROUP + at
        source = pairs_ref[0, slot]
        target = pairs_ref[1, slot]
        used = slot < total
        left = left_ref[pl.ds(pl.multiple_of(source * width, 8), width), :]
        right = right_ref[pl.ds(pl.multiple_of(target * width, 8), width), :]
        if force:
            still = pair_product(left[0:32], right[0:24], right[24:32])
            moved = pair_product(left[32:64], right[32:56], right[56:64])
        else:
            still = pair_product(left, right[0:24], right[24:48])
        highs, lows = [], []
        column_sum = None
        for begin in range(0, pts, rows):
            cut = slice(begin, begin + rows)
            length_sq = jnp.maximum(still[cut, 0:pts], TINY)
            deformed_sq = jnp.maximum(moved[cut, 0:pts] if force else still[cut, pts:], TINY)
            length = length_sq * lax.rsqrt(length_sq)
            extension = deformed_sq * lax.rsqrt(deformed_sq) - length
            weight = weight_ref[at, cut, :]
            if first:
                p = lax.broadcasted_iota(jnp.int32, (rows, pts), 0) + begin
                q = lax.broadcasted_iota(jnp.int32, (rows, pts), 1)
                margin = jnp.where(source == target, 0, -2 * pts)
                weight = jnp.where(p + margin < q, weight.astype(jnp.float32), 0.0)
                weight = weight * jnp.exp2(-length_sq)
                kept_ref[at, cut, :] = weight
            if force:
                state = still[cut, pts:] * length + moved[cut, pts:] * extension
                term = weight * state * lax.rsqrt(deformed_sq + SOFTEN * LOG2E)
            else:
                term = weight * length * extension
                part = jnp.sum(term.reshape(rows // 8, 8, pts), axis=0)
                column_sum = part if column_sum is None else column_sum + part
            high, low = halves(term)
            highs.append(high)
            lows.append(low)
        high = jnp.concatenate(highs, axis=0)
        low = jnp.concatenate(lows, axis=0)
        wide = jnp.concatenate([high, low], axis=1)
        across = (((1,), (1,)), ((), ()))
        if force:
            tall = jnp.concatenate([high, low], axis=0)
            target_rows = right[32:48].astype(jnp.bfloat16)
            begin = pl.multiple_of(source * width, 8) + 32
            source_rows = right_ref[pl.ds(begin, 16), :].astype(jnp.bfloat16)
            to_source = lax.dot_general(
                jnp.concatenate([target_rows, target_rows], axis=1),
                wide,
                across,
                preferred_element_type=jnp.float32,
            )
            to_target = jnp.dot(
                jnp.concatenate([source_rows, source_rows], axis=1),
                tall,
                preferred_element_type=jnp.float32,
            )
        else:
            pick = (lax.broadcasted_iota(jnp.int32, (16, 2 * pts), 0) == 0).astype(jnp.bfloat16)
            to_source = lax.dot_general(pick, wide, across, preferred_element_type=jnp.float32)[0:8]
            to_target = column_sum
        return (
            jnp.where(used, source, extent) * depth,
            jnp.where(used, target, extent) * depth,
            to_source,
            to_target,
        )

    @pl.when(step * GROUP < total)
    def _():
        def turn(index, carry):
            found = [one_slot(index * UNROLL + k) for k in range(UNROLL)]
            for source, target, to_source, to_target in found:
                acc_ref[pl.ds(pl.multiple_of(source, 8), depth), :] += to_source
                acc_ref[pl.ds(pl.multiple_of(target, 8), depth), :] += to_target
            return carry

        lax.fori_loop(0, GROUP // UNROLL, turn, 0)

    @pl.when(step == pl.num_programs(0) - 1)
    def _():
        def finish(chunk, carry):
            at = pl.ds(pl.multiple_of(chunk * 8, 8), 8)

            def row(k):
                return acc_ref[pl.ds(chunk * (8 * depth) + k, 8, stride=depth), :]

            if force:
                count = row(9)
                for k in range(3):
                    moment = row(k) + row(3 + k) + row(6 + k)
                    out_ref[k, at, :] = (moment - current_ref[k, at, :] * count) * (1.0 / SCALE)
            else:
                out_ref[0, at, :] = sum(row(k) for k in range(1, 8)) + row(0)
            return carry

        lax.fori_loop(0, extent // 8, finish, 0)


def run_pass(force, first, pairs, counts, weight, *point_data):
    slots, pts = weight.shape[0], weight.shape[-1]
    extent = point_data[0].shape[1]
    out_rows = 3 if force else 1
    width, depth = (64, 16) if force else (48, 8)

    def slab(i, pairs_ref, count_ref):
        last = (count_ref[1] + GROUP - 1) // GROUP - 1
        return (jnp.minimum(i, last), 0, 0)

    def whole(*_):
        return (0, 0, 0)

    in_specs = [pl.BlockSpec((GROUP, pts, pts), slab)]
    in_specs += [pl.BlockSpec(x.shape, whole, pipeline_mode=pl.Buffered(1)) for x in point_data]
    out_shape = [jax.ShapeDtypeStruct((out_rows, extent, pts), jnp.float32)]
    out_specs = [pl.BlockSpec((out_rows, extent, pts), whole)]
    if first:
        out_shape.append(jax.ShapeDtypeStruct(weight.shape, jnp.float32))
        out_specs.append(pl.BlockSpec((GROUP, pts, pts), slab))
    return pl.pallas_call(
        functools.partial(pass_kernel, force, first),
        grid_spec=pltpu.PrefetchScalarGridSpec(
            num_scalar_prefetch=2,
            grid=(slots // GROUP,),
            in_specs=in_specs,
            out_specs=out_specs,
            scratch_shapes=[
                pltpu.VMEM((extent * width, pts), jnp.float32),
                pltpu.VMEM((extent * width, pts), jnp.float32),
                pltpu.VMEM(((extent + 1) * depth, pts), jnp.float32),
            ],
        ),
        out_shape=out_shape,
        compiler_params=pltpu.CompilerParams(
            dimension_semantics=("arbitrary",), vmem_limit_bytes=48 * 1024 * 1024
        ),
        name="force_pass" if force else "dilatation_pass",
    )(pairs, counts, weight, *point_data)


def body(
    position, displacement, velocity, bulk, shear, volume, edges, block_pairs, block_counts, damage
):
    points = damage.shape[-1]
    clusters = position.shape[-1] // points
    facing = edges.shape[-1]

    def rows_of(quantity):
        return quantity.reshape(-1, clusters, points)

    vol, bulk_c, shear_c = rows_of(volume), rows_of(bulk), rows_of(shear)
    table = jnp.concatenate(
        [
            rows_of(position),
            rows_of(displacement),
            rows_of(velocity),
            (3.0 * bulk_c - 5.0 * shear_c) / vol,
            15.0 * shear_c / vol,
            vol,
        ],
        axis=0,
    )
    pairs = block_pairs[0, 0]
    counts = block_counts[0, 0]
    weight = damage[0, 0]
    hot = (edges[0, 0].reshape(-1)[:, None] == jnp.arange(clusters, dtype=jnp.int32)).astype(
        jnp.float32
    )

    def select(matrix, values):
        return jnp.stack(
            [jnp.dot(matrix, value, precision=lax.Precision.HIGHEST) for value in values]
        )

    def pull(local):
        rows = select(hot, local)
        return jnp.concatenate(
            [from_behind(rows[:, :facing], "circ", -1), shifted(rows[:, facing:], "axial", -1)],
            axis=1,
        )

    def push(halo):
        rows = jnp.concatenate(
            [from_behind(halo[:, :facing], "circ", 1), shifted(halo[:, facing:], "axial", 1)],
            axis=1,
        )
        return select(hot.T, rows)

    def exchanged(partials, last):
        own, halo = partials[:, :clusters], partials[:, clusters:]
        own_sum = own + push(halo)
        halo_sum = halo if last else halo + pull(own)
        return jnp.concatenate([own_sum, halo_sum], axis=1)

    full = jnp.concatenate([table, pull(table)], axis=1)
    place, moving, speed = full[0:3], full[3:6], full[6:9]
    dil_coef, dev_coef, vol = full[9:10], full[10:11], full[11:12]
    vol = jnp.where(vol == 0.0, 1.0, vol)
    still = place * SCALE
    for step in range(TIME_STEPS):
        current = (place + moving) * SCALE
        results = run_pass(False, step == 0, pairs, counts, weight, still, current)
        if step == 0:
            weight = results[1]
        theta = (3.0 / LOG2E) * exchanged(results[0], False) / vol
        coef = jnp.concatenate([dil_coef * theta, dev_coef], axis=0)
        (partials,) = run_pass(True, False, pairs, counts, weight, still, current, coef)
        force = exchanged(partials, step == TIME_STEPS - 1)
        speed = speed + TIMESTEP * force
        moving = moving + TIMESTEP * speed
    return (
        moving[:, :clusters].reshape(displacement.shape),
        speed[:, :clusters].reshape(velocity.shape),
        theta[:, :clusters].reshape(volume.shape),
    )


def solution(mesh):
    wide = P(None, "circ", "axial", None)
    flat = P("circ", "axial", None)
    pairs = P("circ", "axial", None, None)
    return jax.shard_map(
        body,
        mesh=mesh,
        in_specs=(wide, wide, wide, flat, flat, flat, pairs, pairs, flat, P("circ", "axial", None, None, None)),
        out_specs=(wide, wide, flat),
        check_vma=False,
    )
```

time: 783 us -> 308 us (0.39)
  the two profiles are of different devices: /device:TPU:4 before, /device:TPU:18 now
where the time goes in v1:
time: 308 us; the launch traced here: 304 us
  Pallas kernels  250 us (81%)
  starting transfers between devices  24.1 us (8%)
  waiting for transfers between devices  15.8 us (5%)
  matrix products  6.27 us (2%)
  local copies, waits for them, and re-layouts  5.01 us (2%)
    pallas_call x4, Pallas kernels, run_pass(): pl.pallas_call(functools.partial(pass_kernel, force, first), grid_spec=pl...  250 us
    ppermute x8, starting transfers between devices, shifted(): return lax.ppermute(shard, axis, pairs)  17.2 us
    ppermute x8, waiting for transfers between devices, shifted(): return lax.ppermute(shard, axis, pairs)  10.6 us
    ppermute x8, starting transfers between devices, from_behind(): lax.ppermute(block, axis, [((i - distance) % size, i) for i in range(size)])  6.93 us
    dot_general x25, matrix products, select(): jnp.dot(matrix, value, precision=lax.Precision.HIGHEST)  6.27 us
  transfers between devices with their start and end apart: 16, of which 7 were waited for; matrix products, arithmetic and copies ran while one was open for 1% of the time, Pallas kernels for 0%

profile of v1, /device:TPU:18, one launch (start us, length us, event | category | flops | bytes accessed | tf_op | source)
XLA Modules:
  0.0 303.5 jit_solution(1784110647791338064)
XLA Ops:
  1.4 0.9 fusion.63
  2.4 0.9 fusion.62
  3.3 0.9 fusion.61
  7.7 1.9 collective-permute-start.1
  9.8 4.1 %collective-permute-done = f32[12,32,128]{2,1,0:T(8,128)S(1)} collective-permute-done((f32[12,32,128]{2,1,0:T(8,128)S(1)}, f32[12,32,128]{2,1,0:T(8,128)S(1)}, u32[]{:S(2)}, u32[]{:S(2)}) %collective-permute-start) | collective-permute-done | bytes 196640 | tf_op jit(solution)/shard_map/ppermute | solution.py:23
  14.7 43.1 %dilatation_pass.2 = (f32[1,192,128]{2,1,0:T(8,128)S(1)}, f32[320,128,128]{2,1,0:T(8,128)}) custom-call(s32[2,320]{1,0:T(2,128)S(1)} %bitcast.151, s32[2]{0:T(128)S(1)} %bitcast.155, s32[320,128,128]{2,1,0:T(8,128)} %bitcast.159, f32[3,192,128]{2,1,0:T(8,128)S(1)} %get-tuple-element.23.place_ref, f32[3,192,128]{2,1,0:T(8,128)S(1)} %get-tuple-element.22.current_ref), custom_call_target="tpu_custom_call" | custom-call | tf_op jit(solution)/shard_map/dilatation_pass/pallas_call | solution.py:229
  58.5 2.4 collective-permute-start.5
  61.0 1.6 collective-permute-start.2
  62.6 2.1 collective-permute-start.3
  64.8 2.9 collective-permute-done.3
  68.0 83.1 %force_pass.2 = f32[3,192,128]{2,1,0:T(8,128)S(1)} custom-call(s32[2,320]{1,0:T(2,128)S(1)} %bitcast.152, s32[2]{0:T(128)S(1)} %bitcast.156, f32[320,128,128]{2,1,0:T(8,128)} %get-tuple-element.5.weight_ref, f32[3,192,128]{2,1,0:T(8,128)S(1)} %get-tuple-element.23.place_ref, f32[3,192,128]{2,1,0:T(8,128)S(1)} %get-tuple-element.22.current_ref, ...), custom_call_target="tpu_custom_call" | custom-call | tf_op jit(solution)/shard_map/force_pass/pallas_call | solution.py:229
  151.9 2.1 collective-permute-start.8
  154.0 1.9 collective-permute-start.9
  155.9 2.4 collective-permute-start.7
  158.3 3.0 collective-permute-done.7
  162.5 40.2 %dilatation_pass.3 = f32[1,192,128]{2,1,0:T(8,128)S(1)} custom-call(s32[2,320]{1,0:T(2,128)S(1)} %bitcast.153, s32[2]{0:T(128)S(1)} %bitcast.157, f32[320,128,128]{2,1,0:T(8,128)} %get-tuple-element.5.weight_ref, f32[3,192,128]{2,1,0:T(8,128)S(1)} %get-tuple-element.23.place_ref, f32[3,192,128]{2,1,0:T(8,128)S(1)} %get-tuple-element.15.current_ref), custom_call_target="tpu_custom_call" | custom-call | tf_op jit(solution)/shard_map/dilatation_pass/pallas_call | solution.py:229
  203.4 1.9 collective-permute-start.13
  205.4 1.6 collective-permute-start.10
  207.0 2.1 collective-permute-start.11
  209.2 2.9 collective-permute-done.11
  212.4 83.1 %force_pass.3 = f32[3,192,128]{2,1,0:T(8,128)S(1)} custom-call(s32[2,320]{1,0:T(2,128)S(1)} %bitcast.154, s32[2]{0:T(128)S(1)} %bitcast.158, f32[320,128,128]{2,1,0:T(8,128)} %get-tuple-element.5.weight_ref, f32[3,192,128]{2,1,0:T(8,128)S(1)} %get-tuple-element.23.place_ref, f32[3,192,128]{2,1,0:T(8,128)S(1)} %get-tuple-element.15.current_ref, ...), custom_call_target="tpu_custom_call" | custom-call | tf_op jit(solution)/shard_map/force_pass/pallas_call | solution.py:229
  296.3 2.5 collective-permute-start.15
  298.7 1.1 collective-permute-done.14
  299.8 1.8 collective-permute-done.15
  (93 shorter events, 11.7 us)
Async XLA Ops:
  0.6 3.6 %copy-start.6 = (f32[1,1,16384]{2,1,0:T(1,128)S(1)}, f32[1,1,16384]{2,1,0:T(1,128)}, u32[]{:S(2)}) copy-start(f32[1,1,16384]{2,1,0:T(1,128)} %param.14) | copy-start | bytes 196612
  0.6 3.6 %copy-start.7 = (f32[1,1,16384]{2,1,0:T(1,128)S(1)}, f32[1,1,16384]{2,1,0:T(1,128)}, u32[]{:S(2)}) copy-start(f32[1,1,16384]{2,1,0:T(1,128)} %param.13) | copy-start | bytes 196612
  1.4 5.0 %copy-start.2 = (f32[1,1,16384]{2,1,0:T(1,128)S(1)}, f32[1,1,16384]{2,1,0:T(1,128)}, u32[]{:S(2)}) copy-start(f32[1,1,16384]{2,1,0:T(1,128)} %param.15) | copy-start | bytes 196612
  4.4 5.2 %copy-start.3 = (f32[3,1,1,16384]{3,2,1,0:T(1,128)S(1)}, f32[3,1,1,16384]{3,2,1,0:T(1,128)}, u32[]{:S(2)}) copy-start(f32[3,1,1,16384]{3,2,1,0:T(1,128)} %param.10) | copy-start | bytes 589828
  5.1 4.6 %copy-start.4 = (f32[3,1,1,16384]{3,2,1,0:T(1,128)S(1)}, f32[3,1,1,16384]{3,2,1,0:T(1,128)}, u32[]{:S(2)}) copy-start(f32[3,1,1,16384]{3,2,1,0:T(1,128)} %param.11) | copy-start | bytes 589828
  6.0 3.7 %copy-start.5 = (f32[3,1,1,16384]{3,2,1,0:T(1,128)S(1)}, f32[3,1,1,16384]{3,2,1,0:T(1,128)}, u32[]{:S(2)}) copy-start(f32[3,1,1,16384]{3,2,1,0:T(1,128)} %param.12) | copy-start | bytes 589828
  7.2 6.7 %collective-permute-start = (f32[12,32,128]{2,1,0:T(8,128)S(1)}, f32[12,32,128]{2,1,0:T(8,128)S(1)}, u32[]{:S(2)}, u32[]{:S(2)}) collective-permute-start(f32[12,32,128]{2,1,0:T(8,128)S(1)} %get-tuple-element.24), channel_id=1, source_target_pairs={{8,0},{16,8},{24,16},{0,24},{9,1},{17,9},{25,17},{1,25},{10,2},{18... | collective-permute-start | bytes 589832 | tf_op jit(solution)/shard_map/ppermute | solution.py:23
  7.7 6.2 %collective-permute-start.1 = (f32[12,32,128]{2,1,0:T(8,128)S(1)}, f32[12,32,128]{2,1,0:T(8,128)S(1)}, u32[]{:S(2)}, u32[]{:S(2)}) collective-permute-start(f32[12,32,128]{2,1,0:T(8,128)S(1)} %get-tuple-element.25), channel_id=1, source_target_pairs={{1,0},{2,1},{3,2},{4,3},{5,4},{6,5},{7,6},{9,8},{10,9},{11,10},{12... | collective-permute-start | bytes 589832 | tf_op jit(solution)/shard_map/ppermute | solution.py:29
  14.0 0.7 copy-start
  14.0 0.7 copy-start.1
  58.0 6.6 %collective-permute-start.4 = (f32[1,32,128]{2,1,0:T(8,128)S(1)}, f32[1,32,128]{2,1,0:T(8,128)S(1)}, u32[]{:S(2)}, u32[]{:S(2)}) collective-permute-start(f32[1,32,128]{2,1,0:T(8,128)S(1)} %get-tuple-element.51), channel_id=1, source_target_pairs={{8,0},{16,8},{24,16},{0,24},{9,1},{17,9},{25,17},{1,25},{10,2},{18... | collective-permute-start | bytes 49160 | tf_op jit(solution)/shard_map/ppermute | solution.py:23
  58.5 6.1 %collective-permute-start.5 = (f32[1,32,128]{2,1,0:T(8,128)S(1)}, f32[1,32,128]{2,1,0:T(8,128)S(1)}, u32[]{:S(2)}, u32[]{:S(2)}) collective-permute-start(f32[1,32,128]{2,1,0:T(8,128)S(1)} %get-tuple-element.52), channel_id=1, source_target_pairs={{1,0},{2,1},{3,2},{4,3},{5,4},{6,5},{7,6},{9,8},{10,9},{11,10},{12... | collective-permute-start | bytes 49160 | tf_op jit(solution)/shard_map/ppermute | solution.py:29
  61.0 3.8 %collective-permute-start.2 = (f32[1,32,128]{2,1,0:T(8,128)S(1)}, f32[1,32,128]{2,1,0:T(8,128)S(1)}, u32[]{:S(2)}, u32[]{:S(2)}) collective-permute-start(f32[1,32,128]{2,1,0:T(8,128)S(1)} %get-tuple-element.45), channel_id=1, source_target_pairs={{24,0},{0,8},{8,16},{16,24},{25,1},{1,9},{9,17},{17,25},{26,2},{2,... | collective-permute-start | bytes 49160 | tf_op jit(solution)/shard_map/ppermute | solution.py:23
  62.6 5.0 %collective-permute-start.3 = (f32[1,32,128]{2,1,0:T(8,128)S(1)}, f32[1,32,128]{2,1,0:T(8,128)S(1)}, u32[]{:S(2)}, u32[]{:S(2)}) collective-permute-start(f32[1,32,128]{2,1,0:T(8,128)S(1)} %get-tuple-element.46), channel_id=1, source_target_pairs={{0,1},{1,2},{2,3},{3,4},{4,5},{5,6},{6,7},{8,9},{9,10},{10,11},{11... | collective-permute-start | bytes 49160 | tf_op jit(solution)/shard_map/ppermute | solution.py:29
  151.8 6.5 %collective-permute-start.6 = (f32[3,32,128]{2,1,0:T(8,128)S(1)}, f32[3,32,128]{2,1,0:T(8,128)S(1)}, u32[]{:S(2)}, u32[]{:S(2)}) collective-permute-start(f32[3,32,128]{2,1,0:T(8,128)S(1)} %get-tuple-element.31), channel_id=1, source_target_pairs={{24,0},{0,8},{8,16},{16,24},{25,1},{1,9},{9,17},{17,25},{26,2},{2,... | collective-permute-start | bytes 147464 | tf_op jit(solution)/shard_map/ppermute | solution.py:23
  151.9 10.4 %collective-permute-start.8 = (f32[3,32,128]{2,1,0:T(8,128)S(1)}, f32[3,32,128]{2,1,0:T(8,128)S(1)}, u32[]{:S(2)}, u32[]{:S(2)}) collective-permute-start(f32[3,32,128]{2,1,0:T(8,128)S(1)} %get-tuple-element.43), channel_id=1, source_target_pairs={{8,0},{16,8},{24,16},{0,24},{9,1},{17,9},{25,17},{1,25},{10,2},{18... | collective-permute-start | bytes 147464 | tf_op jit(solution)/shard_map/ppermute | solution.py:23
  154.0 8.3 %collective-permute-start.9 = (f32[3,32,128]{2,1,0:T(8,128)S(1)}, f32[3,32,128]{2,1,0:T(8,128)S(1)}, u32[]{:S(2)}, u32[]{:S(2)}) collective-permute-start(f32[3,32,128]{2,1,0:T(8,128)S(1)} %get-tuple-element.44), channel_id=1, source_target_pairs={{1,0},{2,1},{3,2},{4,3},{5,4},{6,5},{7,6},{9,8},{10,9},{11,10},{12... | collective-permute-start | bytes 147464 | tf_op jit(solution)/shard_map/ppermute | solution.py:29
  155.9 5.4 %collective-permute-start.7 = (f32[3,32,128]{2,1,0:T(8,128)S(1)}, f32[3,32,128]{2,1,0:T(8,128)S(1)}, u32[]{:S(2)}, u32[]{:S(2)}) collective-permute-start(f32[3,32,128]{2,1,0:T(8,128)S(1)} %get-tuple-element.30), channel_id=1, source_target_pairs={{0,1},{1,2},{2,3},{3,4},{4,5},{5,6},{6,7},{8,9},{9,10},{10,11},{11... | collective-permute-start | bytes 147464 | tf_op jit(solution)/shard_map/ppermute | solution.py:29
  202.9 6.2 %collective-permute-start.12 = (f32[1,32,128]{2,1,0:T(8,128)S(1)}, f32[1,32,128]{2,1,0:T(8,128)S(1)}, u32[]{:S(2)}, u32[]{:S(2)}) collective-permute-start(f32[1,32,128]{2,1,0:T(8,128)S(1)} %get-tuple-element.49), channel_id=1, source_target_pairs={{8,0},{16,8},{24,16},{0,24},{9,1},{17,9},{25,17},{1,25},{10,2},{18... | collective-permute-start | bytes 49160 | tf_op jit(solution)/shard_map/ppermute | solution.py:23
  203.4 5.7 %collective-permute-start.13 = (f32[1,32,128]{2,1,0:T(8,128)S(1)}, f32[1,32,128]{2,1,0:T(8,128)S(1)}, u32[]{:S(2)}, u32[]{:S(2)}) collective-permute-start(f32[1,32,128]{2,1,0:T(8,128)S(1)} %get-tuple-element.50), channel_id=1, source_target_pairs={{1,0},{2,1},{3,2},{4,3},{5,4},{6,5},{7,6},{9,8},{10,9},{11,10},{12... | collective-permute-start | bytes 49160 | tf_op jit(solution)/shard_map/ppermute | solution.py:29
  205.4 3.8 %collective-permute-start.10 = (f32[1,32,128]{2,1,0:T(8,128)S(1)}, f32[1,32,128]{2,1,0:T(8,128)S(1)}, u32[]{:S(2)}, u32[]{:S(2)}) collective-permute-start(f32[1,32,128]{2,1,0:T(8,128)S(1)} %get-tuple-element.41), channel_id=1, source_target_pairs={{24,0},{0,8},{8,16},{16,24},{25,1},{1,9},{9,17},{17,25},{26,2},{2,... | collective-permute-start | bytes 49160 | tf_op jit(solution)/shard_map/ppermute | solution.py:23
  207.0 5.0 %collective-permute-start.11 = (f32[1,32,128]{2,1,0:T(8,128)S(1)}, f32[1,32,128]{2,1,0:T(8,128)S(1)}, u32[]{:S(2)}, u32[]{:S(2)}) collective-permute-start(f32[1,32,128]{2,1,0:T(8,128)S(1)} %get-tuple-element.42), channel_id=1, source_target_pairs={{0,1},{1,2},{2,3},{3,4},{4,5},{5,6},{6,7},{8,9},{9,10},{10,11},{11... | collective-permute-start | bytes 49160 | tf_op jit(solution)/shard_map/ppermute | solution.py:29
  295.5 4.3 %collective-permute-start.14 = (f32[3,32,128]{2,1,0:T(8,128)S(1)}, f32[3,32,128]{2,1,0:T(8,128)S(1)}, u32[]{:S(2)}, u32[]{:S(2)}) collective-permute-start(f32[3,32,128]{2,1,0:T(8,128)S(1)} %get-tuple-element.29), channel_id=1, source_target_pairs={{24,0},{0,8},{8,16},{16,24},{25,1},{1,9},{9,17},{17,25},{26,2},{2,... | collective-permute-start | bytes 147464 | tf_op jit(solution)/shard_map/ppermute | solution.py:23
  296.3 5.4 %collective-permute-start.15 = (f32[3,32,128]{2,1,0:T(8,128)S(1)}, f32[3,32,128]{2,1,0:T(8,128)S(1)}, u32[]{:S(2)}, u32[]{:S(2)}) collective-permute-start(f32[3,32,128]{2,1,0:T(8,128)S(1)} %get-tuple-element.28), channel_id=1, source_target_pairs={{0,1},{1,2},{2,3},{3,4},{4,5},{5,6},{6,7},{8,9},{9,10},{10,11},{11... | collective-permute-start | bytes 147464 | tf_op jit(solution)/shard_map/ppermute | solution.py:29

commit v2 on v1

--- a/solution.py
+++ b/solution.py
@@ -15,18 +15,90 @@
 SCALE = math.sqrt(LOG2E)
 TINY = 1e-12
 GROUP = 16
-UNROLL = 4
-
-
-def from_behind(block, axis, distance):
-    size = lax.axis_size(axis)
-    return lax.ppermute(block, axis, [((i - distance) % size, i) for i in range(size)])
-
-
-def shifted(shard, axis, by):
-    size = lax.axis_size(axis)
-    pairs = [(i, i + by) for i in range(size) if 0 <= i + by < size]
-    return lax.ppermute(shard, axis, pairs)
+UNROLL = 8
+
+
+def exact_rows(matrix, values):
+    parts = jnp.concatenate([x.astype(jnp.bfloat16) for x in split3(values)], axis=0)
+    return jnp.dot(matrix, parts, preferred_element_type=jnp.float32)
+
+
+def exchange_kernel(part_ref, hot_ref, hot_t_ref, out_ref, send_buf, recv_buf, send_sem, recv_sem):
+    circ, axial = lax.axis_index("circ"), lax.axis_index("axial")
+    circs, axials = lax.axis_size("circ"), lax.axis_size("axial")
+    targets = [
+        {"circ": lax.rem(circ + circs - 1, circs)},
+        {"axial": lax.rem(axial + axials - 1, axials)},
+        {"circ": lax.rem(circ + 1, circs)},
+        {"axial": lax.rem(axial + 1, axials)},
+    ]
+    barrier = pltpu.get_barrier_semaphore()
+    for device in targets:
+        pl.semaphore_signal(
+            barrier, inc=1, device_id=device, device_id_type=pl.DeviceIdType.MESH
+        )
+    row_count, _, pts = part_ref.shape
+    clusters = hot_t_ref.shape[0]
+    facing = hot_ref.shape[0] // 2
+
+    def copy(k):
+        return pltpu.make_async_remote_copy(
+            src_ref=send_buf.at[k],
+            dst_ref=recv_buf.at[k],
+            send_sem=send_sem.at[k],
+            recv_sem=recv_sem.at[k],
+            device_id=targets[k],
+            device_id_type=pl.DeviceIdType.MESH,
+        )
+
+    copies = [copy(k) for k in range(4)]
+    send_buf[2] = part_ref[:, clusters : clusters + facing, :]
+    send_buf[3] = part_ref[:, clusters + facing :, :]
+    for r in range(row_count):
+        rows = exact_rows(hot_ref[...], part_ref[r, 0:clusters, :])
+        send_buf[0, r] = rows[:facing]
+        send_buf[1, r] = rows[facing:]
+    pl.semaphore_wait(barrier, 4)
+    for k in (0, 2, 1, 3):
+        copies[k].start()
+    for k in (0, 2, 1, 3):
+        copies[k].wait()
+    has_after = axial < axials - 1
+    has_before = axial > 0
+    for r in range(row_count):
+        halo = part_ref[r, clusters:, :]
+        out_ref[r, clusters : clusters + facing, :] = halo[:facing] + recv_buf[0, r]
+        out_ref[r, clusters + facing :, :] = halo[facing:] + jnp.where(
+            has_after, recv_buf[1, r], 0.0
+        )
+        arrived = jnp.concatenate(
+            [recv_buf[2, r], jnp.where(has_before, recv_buf[3, r], 0.0)], axis=0
+        )
+        out_ref[r, 0:clusters, :] = part_ref[r, 0:clusters, :] + exact_rows(
+            hot_t_ref[...], arrived
+        )
+
+
+def exchange(part, hot, hot_t, collective_id):
+    row_count, _, pts = part.shape
+    facing = hot.shape[0] // 2
+    block = pltpu.VMEM((4, row_count, facing, pts), jnp.float32)
+    return pl.pallas_call(
+        exchange_kernel,
+        out_shape=jax.ShapeDtypeStruct(part.shape, jnp.float32),
+        in_specs=[pl.BlockSpec(memory_space=pltpu.VMEM)] * 3,
+        out_specs=pl.BlockSpec(memory_space=pltpu.VMEM),
+        scratch_shapes=[
+            block,
+            block,
+            pltpu.SemaphoreType.DMA((4,)),
+            pltpu.SemaphoreType.DMA((4,)),
+        ],
+        compiler_params=pltpu.CompilerParams(
+            collective_id=collective_id, has_side_effects=True
+        ),
+        name=f"exchange_{row_count}",
+    )(part, hot, hot_t)
 
 
 def split3(x):
@@ -58,16 +130,10 @@
     return high, low
 
 
-def pair_product(left, right_a, right_b):
+def two_columns(right_a, right_b):
     upper = jnp.concatenate([right_a, jnp.zeros_like(right_a)], axis=1)
     lower = jnp.concatenate([jnp.zeros_like(right_b), right_b], axis=1)
-    both = jnp.concatenate([upper, lower], axis=0).astype(jnp.bfloat16)
-    return lax.dot_general(
-        left.astype(jnp.bfloat16),
-        both,
-        (((0,), (0,)), ((), ())),
-        preferred_element_type=jnp.float32,
-    )
+    return jnp.concatenate([upper, lower], axis=0)
 
 
 def pass_kernel(force, first, pairs_ref, count_ref, weight_ref, place_ref, current_ref, *rest):
@@ -81,8 +147,9 @@
     pts = weight_ref.shape[-1]
     extent = place_ref.shape[1]
     width = left_ref.shape[0] // extent
+    used_rows = 64 if force else 48
     depth = 16 if force else 8
-    rows = 32
+    rows, chunk = 32, 64
 
     @pl.when(step == 0)
     def _():
@@ -98,7 +165,7 @@
                 groups.append(sum_features(coef_ref[1, at, :]))
             left = [x for group in groups for x in group[0]]
             right = [x for group in groups for x in group[1]]
-            for k in range(width):
+            for k in range(used_rows):
                 spot = pl.ds(chunk * (8 * width) + k, 8, stride=width)
                 left_ref[spot, :] = left[k]
                 right_ref[spot, :] = right[k]
@@ -111,19 +178,41 @@
         source = pairs_ref[0, slot]
         target = pairs_ref[1, slot]
         used = slot < total
-        left = left_ref[pl.ds(pl.multiple_of(source * width, 8), width), :]
-        right = right_ref[pl.ds(pl.multiple_of(target * width, 8), width), :]
+        left = left_ref[pl.ds(pl.multiple_of(source * width, 8), used_rows), :]
+        right = right_ref[pl.ds(pl.multiple_of(target * width, 8), used_rows), :]
         if force:
-            still = pair_product(left[0:32], right[0:24], right[24:32])
-            moved = pair_product(left[32:64], right[32:56], right[56:64])
+            turned = jnp.transpose(left).astype(jnp.bfloat16)
+            blank = jnp.zeros((32, 2 * pts), jnp.float32)
+            still_right = jnp.concatenate(
+                [two_columns(right[0:24], right[24:32]), blank], axis=0
+            ).astype(jnp.bfloat16)
+            moved_right = jnp.concatenate(
+                [blank, two_columns(right[32:56], right[56:64])], axis=0
+            ).astype(jnp.bfloat16)
         else:
-            still = pair_product(left, right[0:24], right[24:48])
+            still = lax.dot_general(
+                left.astype(jnp.bfloat16),
+                two_columns(right[0:24], right[24:48]).astype(jnp.bfloat16),
+                (((0,), (0,)), ((), ())),
+                preferred_element_type=jnp.float32,
+            )
         highs, lows = [], []
         column_sum = None
         for begin in range(0, pts, rows):
             cut = slice(begin, begin + rows)
-            length_sq = jnp.maximum(still[cut, 0:pts], TINY)
-            deformed_sq = jnp.maximum(moved[cut, 0:pts] if force else still[cut, pts:], TINY)
+            if force:
+                local = slice(begin % chunk, begin % chunk + rows)
+                if begin % chunk == 0:
+                    points = turned[begin : begin + chunk]
+                    still_cut = jnp.dot(points, still_right, preferred_element_type=jnp.float32)
+                    moved_cut = jnp.dot(points, moved_right, preferred_element_type=jnp.float32)
+                still_rows, moved_rows = still_cut[local], moved_cut[local]
+            else:
+                still_rows = still[cut]
+            length_sq = jnp.maximum(still_rows[:, 0:pts], TINY)
+            deformed_sq = jnp.maximum(
+                moved_rows[:, 0:pts] if force else still_rows[:, pts:], TINY
+            )
             length = length_sq * lax.rsqrt(length_sq)
             extension = deformed_sq * lax.rsqrt(deformed_sq) - length
             weight = weight_ref[at, cut, :]
@@ -135,7 +224,7 @@
                 weight = weight * jnp.exp2(-length_sq)
                 kept_ref[at, cut, :] = weight
             if force:
-                state = still[cut, pts:] * length + moved[cut, pts:] * extension
+                state = still_rows[:, pts:] * length + moved_rows[:, pts:] * extension
                 term = weight * state * lax.rsqrt(deformed_sq + SOFTEN * LOG2E)
             else:
                 term = weight * length * extension
@@ -210,7 +299,7 @@
     slots, pts = weight.shape[0], weight.shape[-1]
     extent = point_data[0].shape[1]
     out_rows = 3 if force else 1
-    width, depth = (64, 16) if force else (48, 8)
+    width, depth = (72, 16) if force else (56, 8)
 
     def slab(i, pairs_ref, count_ref):
         last = (count_ref[1] + GROUP - 1) // GROUP - 1
@@ -273,35 +362,15 @@
     counts = block_counts[0, 0]
     weight = damage[0, 0]
     hot = (edges[0, 0].reshape(-1)[:, None] == jnp.arange(clusters, dtype=jnp.int32)).astype(
-        jnp.float32
+        jnp.bfloat16
     )
 
-    def select(matrix, values):
-        return jnp.stack(
-            [jnp.dot(matrix, value, precision=lax.Precision.HIGHEST) for value in values]
-        )
-
-    def pull(local):
-        rows = select(hot, local)
-        return jnp.concatenate(
-            [from_behind(rows[:, :facing], "circ", -1), shifted(rows[:, facing:], "axial", -1)],
-            axis=1,
-        )
-
-    def push(halo):
-        rows = jnp.concatenate(
-            [from_behind(halo[:, :facing], "circ", 1), shifted(halo[:, facing:], "axial", 1)],
-            axis=1,
-        )
-        return select(hot.T, rows)
-
-    def exchanged(partials, last):
-        own, halo = partials[:, :clusters], partials[:, clusters:]
-        own_sum = own + push(halo)
-        halo_sum = halo if last else halo + pull(own)
-        return jnp.concatenate([own_sum, halo_sum], axis=1)
-
-    full = jnp.concatenate([table, pull(table)], axis=1)
+    hot_t = jnp.concatenate([hot.T] * 3, axis=1)
+    hot = jnp.concatenate([hot] * 3, axis=1)
+    padded = jnp.concatenate(
+        [table, jnp.zeros((table.shape[0], 2 * facing, points), jnp.float32)], axis=1
+    )
+    full = exchange(padded, hot, hot_t, 0)
     place, moving, speed = full[0:3], full[3:6], full[6:9]
     dil_coef, dev_coef, vol = full[9:10], full[10:11], full[11:12]
     vol = jnp.where(vol == 0.0, 1.0, vol)
@@ -311,10 +380,10 @@
         results = run_pass(False, step == 0, pairs, counts, weight, still, current)
         if step == 0:
             weight = results[1]
-        theta = (3.0 / LOG2E) * exchanged(results[0], False) / vol
+        theta = (3.0 / LOG2E) * exchange(results[0], hot, hot_t, 1) / vol
         coef = jnp.concatenate([dil_coef * theta, dev_coef], axis=0)
         (partials,) = run_pass(True, False, pairs, counts, weight, still, current, coef)
-        force = exchanged(partials, step == TIME_STEPS - 1)
+        force = exchange(partials, hot, hot_t, 2)
         speed = speed + TIMESTEP * force
         moving = moving + TIMESTEP * speed
     return (

time: 308 us -> 274 us (0.89)
  the two profiles are of different devices: /device:TPU:18 before, /device:TPU:4 now
where the time goes in v2:
time: 274 us; the launch traced here: 270 us
  Pallas kernels  254 us (93%)
  other arithmetic  8.34 us (3%)
  local copies, waits for them, and re-layouts  7.23 us (3%)
    pallas_call x4, Pallas kernels, run_pass(): pl.pallas_call(functools.partial(pass_kernel, force, first), grid_spec=pl...  161 us
    pallas_call x5, Pallas kernels, exchange(): pl.pallas_call(exchange_kernel, out_shape=jax.ShapeDtypeStruct(part.shape...  93.2 us

profile of v2, /device:TPU:4, one launch (start us, length us, event | category | flops | bytes accessed | tf_op | source)
XLA Modules:
  0.0 270.3 jit_solution(12002580642654350923)
XLA Ops:
  0.7 0.8 eq.28
  2.2 0.7 add_convert_fusion.hot_t_ref
  2.9 1.0 broadcast_multiply_fusion
  3.9 0.9 constant_dynamic-update-slice_fusion.3
  4.9 0.9 constant_dynamic-update-slice_fusion.2
  5.9 1.2 concatenate.23.part_ref
  7.1 17.2 %exchange_12.1 = f32[12,192,128]{2,1,0:T(8,128)} custom-call(f32[12,192,128]{2,1,0:T(8,128)} %concatenate.23.part_ref, bf16[64,384]{1,0:T(8,128)(2,1)} %add_convert_fusion.1.hot_ref, bf16[128,192]{1,0:T(8,128)(2,1)} %add_convert_fusion.hot_t_ref), custom_call_target="tpu_custom_call" | custom-call | tf_op jit(solution)/shard_map/exchange_12/pallas_call | solution.py:86
  24.3 1.1 add_multiply_fusion.1
  25.5 26.7 %dilatation_pass.2 = (f32[1,192,128]{2,1,0:T(8,128)S(1)}, f32[320,128,128]{2,1,0:T(8,128)}) custom-call(s32[2,320]{1,0:T(2,128)S(1)} %bitcast.12, s32[2]{0:T(128)S(1)} %bitcast.16, s32[320,128,128]{2,1,0:T(8,128)} %bitcast.20, f32[3,192,128]{2,1,0:T(8,128)S(1)} %get-tuple-element.20.place_ref, f32[3,192,128]{2,1,0:T(8,128)S(1)} %get-tuple-element.19.current_ref), custom_call_target="tpu_custom_call" | custom-call | tf_op jit(solution)/shard_map/dilatation_pass/pallas_call | solution.py:318
  52.2 0.6 copy-done.3
  52.8 12.1 %exchange_1.2 = f32[1,192,128]{2,1,0:T(8,128)} custom-call(f32[1,192,128]{2,1,0:T(8,128)} %copy-done.3, bf16[64,384]{1,0:T(8,128)(2,1)} %add_convert_fusion.1.hot_ref, bf16[128,192]{1,0:T(8,128)(2,1)} %add_convert_fusion.hot_t_ref), custom_call_target="tpu_custom_call" | custom-call | tf_op jit(solution)/shard_map/exchange_1/pallas_call | solution.py:86
  64.9 0.9 divide_multiply_fusion
  65.9 56.1 %force_pass.2.part_ref = f32[3,192,128]{2,1,0:T(8,128)S(1)} custom-call(s32[2,320]{1,0:T(2,128)S(1)} %bitcast.13, s32[2]{0:T(128)S(1)} %bitcast.17, f32[320,128,128]{2,1,0:T(8,128)} %get-tuple-element.5.weight_ref, f32[3,192,128]{2,1,0:T(8,128)S(1)} %get-tuple-element.20.place_ref, f32[3,192,128]{2,1,0:T(8,128)S(1)} %get-tuple-element.19.current_ref, ...), custom_call_target="tpu_custom_call" | custom-call | tf_op jit(solution)/shard_map/force_pass/pallas_call | solution.py:318
  122.1 0.7 copy-done.1
  122.8 25.7 %exchange_3.2 = f32[3,192,128]{2,1,0:T(8,128)} custom-call(f32[3,192,128]{2,1,0:T(8,128)} %copy-done.1, bf16[64,384]{1,0:T(8,128)(2,1)} %add_convert_fusion.1.hot_ref, bf16[128,192]{1,0:T(8,128)(2,1)} %add_convert_fusion.hot_t_ref), custom_call_target="tpu_custom_call" | custom-call | tf_op jit(solution)/shard_map/exchange_3/pallas_call | solution.py:86
  148.5 1.1 add_multiply_fusion
  149.5 21.7 %dilatation_pass.3.part_ref = f32[1,192,128]{2,1,0:T(8,128)S(1)} custom-call(s32[2,320]{1,0:T(2,128)S(1)} %bitcast.14, s32[2]{0:T(128)S(1)} %bitcast.18, f32[320,128,128]{2,1,0:T(8,128)} %get-tuple-element.5.weight_ref, f32[3,192,128]{2,1,0:T(8,128)S(1)} %get-tuple-element.20.place_ref, f32[3,192,128]{2,1,0:T(8,128)S(1)} %get-tuple-element.15.current_ref), custom_call_target="tpu_custom_call" | custom-call | tf_op jit(solution)/shard_map/dilatation_pass/pallas_call | solution.py:318
  171.9 12.0 %exchange_1.3 = f32[1,192,128]{2,1,0:T(8,128)} custom-call(f32[1,192,128]{2,1,0:T(8,128)} %copy-done.2, bf16[64,384]{1,0:T(8,128)(2,1)} %add_convert_fusion.1.hot_ref, bf16[128,192]{1,0:T(8,128)(2,1)} %add_convert_fusion.hot_t_ref), custom_call_target="tpu_custom_call" | custom-call | tf_op jit(solution)/shard_map/exchange_1/pallas_call | solution.py:86
  183.9 0.9 slice_multiply_fusion.1
  184.8 56.1 %force_pass.3.part_ref = f32[3,192,128]{2,1,0:T(8,128)S(1)} custom-call(s32[2,320]{1,0:T(2,128)S(1)} %bitcast.15, s32[2]{0:T(128)S(1)} %bitcast.19, f32[320,128,128]{2,1,0:T(8,128)} %get-tuple-element.5.weight_ref, f32[3,192,128]{2,1,0:T(8,128)S(1)} %get-tuple-element.20.place_ref, f32[3,192,128]{2,1,0:T(8,128)S(1)} %get-tuple-element.15.current_ref, ...), custom_call_target="tpu_custom_call" | custom-call | tf_op jit(solution)/shard_map/force_pass/pallas_call | solution.py:318
  241.0 0.7 copy-done
  241.7 26.2 %exchange_3.3 = f32[3,192,128]{2,1,0:T(8,128)} custom-call(f32[3,192,128]{2,1,0:T(8,128)} %copy-done, bf16[64,384]{1,0:T(8,128)(2,1)} %add_convert_fusion.1.hot_ref, bf16[128,192]{1,0:T(8,128)(2,1)} %add_convert_fusion.hot_t_ref), custom_call_target="tpu_custom_call" | custom-call | tf_op jit(solution)/shard_map/exchange_3/pallas_call | solution.py:86
  267.9 1.0 multiply_add_fusion
  268.9 0.8 fusion
  (27 shorter events, 2.1 us)
Async XLA Ops:
  0.6 5.2 %copy-start.8 = (f32[1,1,16384]{2,1,0:T(1,128)S(1)}, f32[1,1,16384]{2,1,0:T(1,128)}, u32[]{:S(2)}) copy-start(f32[1,1,16384]{2,1,0:T(1,128)} %param.15) | copy-start | bytes 196612
  0.6 5.2 %copy-start.9 = (f32[3,1,1,16384]{3,2,1,0:T(1,128)S(1)}, f32[3,1,1,16384]{3,2,1,0:T(1,128)}, u32[]{:S(2)}) copy-start(f32[3,1,1,16384]{3,2,1,0:T(1,128)} %param.12) | copy-start | bytes 589828
  24.3 1.1 copy-start.4
  24.3 1.1 copy-start.5
  25.4 39.5 %copy-start.6 = (f32[12,192,128]{2,1,0:T(8,128)S(1)}, f32[12,192,128]{2,1,0:T(8,128)}, u32[]{:S(2)}) copy-start(f32[12,192,128]{2,1,0:T(8,128)} %exchange_12.1) | copy-start | bytes 3538948
  52.2 0.6 copy-start.3
  122.0 0.7 copy-start.1
  171.2 0.6 copy-start.2
  184.8 83.1 %copy-start.7 = (f32[3,192,128]{2,1,0:T(8,128)S(1)}, f32[3,192,128]{2,1,0:T(8,128)}, u32[]{:S(2)}) copy-start(f32[3,192,128]{2,1,0:T(8,128)} %exchange_3.2) | copy-start | bytes 884740
  241.0 0.7 copy-start
